TPU v7x, 32 devices: a whole 2x2x4 slice. The times are simulated.
32 devices in a mesh: slab: 8 (over y, x, core), col: 4 (over z).
Axes of the slice: x: 2, y: 2, z: 4, core: 2. Of those that a mesh axis runs over, the one named last changes fastest.
Arguments:
- rest_points: float32 [3, 8, 8, 128], P(None, 'slab', 'col'), may hold values from 0 to 8, as said below
- tile_fill: int32 [8, 8], P('slab', 'col'), may hold values from 32 to 128, as said below
- displacement: float32 [3, 8, 8, 128], P(None, 'slab', 'col'), may hold values from -0.6 to 0.6
- velocity: float32 [3, 8, 8, 128], P(None, 'slab', 'col'), may hold values from -0.6 to 0.6
- back_extension: bfloat16 [2, 8, 8, 9, 128, 128], P(None, 'slab', 'col'), may hold values from -0.59765625 to 0.59765625
Outputs:
- displacement_out: float32 [3, 8, 8, 128], P(None, 'slab', 'col')
- velocity_out: float32 [3, 8, 8, 128], P(None, 'slab', 'col')
- back_extension_out: bfloat16 [2, 8, 8, 9, 128, 128], P(None, 'slab', 'col')
Inputs may be any that keep to these rules, and one draw needn't show every extreme that they name: `tile_fill`: point slots of a tile are filled from the first one; at least a quarter of the 128 slots are live. `rest_points`: the points of tile (r, c) lie in its unit box: r plus [0, 1) along the first component, c plus [0, 1) along the second, [0, 1) along the third.
All inputs are finite; a program needn't handle non-finite values.
Results may differ from a plain program's by a relative error of at most 0.0051.
Values sent between devices are 32-bit elements; how exact they have to be, the bound alone decides.
A program may use at most 128 MiB of HBM per device.

v0:
```python
import jax
import jax.numpy as jnp
from jax import lax
from jax.sharding import PartitionSpec as P

STEPS = 2


stencil_offsets = [(-1, -1), (-1, 0), (-1, 1), (0, -1), (0, 0), (0, 1), (1, -1), (1, 0), (1, 1)]


def passed_along(value, axis, steps):
    count = lax.axis_size(axis)
    leading, last = (max(0, -steps), min(count, count - steps))
    return lax.ppermute(value, axis, [(source, source + steps) for source in range(leading, last)])


def with_halo(array, sides, width):
    for axis, dim in sides:
        peers, length = (lax.axis_size(axis), array.shape[dim])
        up = [(i, (i + 1) % peers) for i in range(peers - 1)]
        down = [(j, i) for i, j in up]
        last = lax.slice_in_dim(array, length - width, length, axis=dim)
        leading = lax.slice_in_dim(array, 0, width, axis=dim)
        before = lax.ppermute(last, axis, up)
        after = lax.ppermute(leading, axis, down)
        array = jnp.concatenate([before, array, after], axis=dim)
    return array


def pair_geometry(rest_halo, alive_halo, rows, cols, row_shift, col_shift):
    home_side = rest_halo[:, 1 : 1 + rows, 1 : 1 + cols, :, None]
    far_side = rest_halo[
        :, 1 + row_shift : 1 + row_shift + rows, 1 + col_shift : 1 + col_shift + cols, None, :
    ]
    bond = far_side - home_side
    length = jnp.sqrt(jnp.sum(bond * bond, axis=0))
    closeness = jnp.maximum(1.0 - length, 0.0)
    weight = closeness * closeness * alive_halo[1 : 1 + rows, 1 : 1 + cols, :, None]
    weight = (
        weight
        * alive_halo[
            1 + row_shift : 1 + row_shift + rows, 1 + col_shift : 1 + col_shift + cols, None, :
        ]
    )
    if row_shift == 0 and col_shift == 0:
        weight = weight * (1.0 - jnp.eye(weight.shape[-1], dtype=jnp.float32))
    return (length, weight)


def deformed(place_halo, length, rows, cols, row_shift, col_shift):
    home_side = place_halo[:, 1 : 1 + rows, 1 : 1 + cols, :, None]
    far_side = place_halo[
        :, 1 + row_shift : 1 + row_shift + rows, 1 + col_shift : 1 + col_shift + cols, None, :
    ]
    separation = far_side - home_side
    squared = jnp.sum(separation * separation, axis=0)
    stretch = jnp.sqrt(squared) - length
    bearing = separation * jax.lax.rsqrt(squared + 0.01)
    return (stretch, bearing)


def return_across(edge, offset):
    return passed_along(edge, "col", offset)


def return_along(edge, offset):
    return passed_along(edge, "slab", offset)


def per_device(rest_points, tile_fill, displacement, velocity, back_extension):
    rows, cols, points = (rest_points.shape[1], rest_points.shape[2], rest_points.shape[3])
    alive = (jnp.arange(points, dtype=jnp.int32)[None, None, :] < tile_fill[:, :, None]).astype(
        jnp.float32
    )
    joined = jnp.concatenate([rest_points, alive[None]], 0)
    joined_halo = with_halo(joined, (("slab", 1), ("col", 2)), 1)
    rest_halo = joined_halo[:3]
    alive_halo = joined_halo[3]
    geometry = [
        pair_geometry(rest_halo, alive_halo, rows, cols, rs, cs) for rs, cs in stencil_offsets
    ]
    volume = jnp.zeros((rows, cols, points), jnp.float32)
    for length, weight in geometry:
        volume = volume + jnp.sum(weight * length * length, axis=-1)
    volume = jnp.maximum(volume, 1.0)
    history = back_extension
    for step_index in range(STEPS):
        moved_halo = with_halo(displacement, (("slab", 1), ("col", 2)), 1)
        place_halo = rest_halo + moved_halo
        shapes = [
            deformed(place_halo, geometry[index][0], rows, cols, rs, cs)
            for index, (rs, cs) in enumerate(stencil_offsets)
        ]
        dilatation = jnp.zeros((rows, cols, points), jnp.float32)
        for index in range(9):
            length, weight = geometry[index]
            dilatation = dilatation + jnp.sum(weight * length * shapes[index][0], axis=-1)
        dilatation = 3.0 * dilatation / volume
        forces, first_states, second_states = ([], [], [])
        for index in range(9):
            length, weight = geometry[index]
            deviator = shapes[index][0] - dilatation[..., None] * length / 3.0
            back_one = 0.6 * history[0, :, :, index].astype(jnp.float32) + 0.4 * deviator
            back_two = 0.95 * history[1, :, :, index].astype(jnp.float32) + 0.05 * deviator
            bond_force = 3.0 * dilatation[..., None] * weight * length / volume[..., None]
            bond_force = bond_force + 7.5 * weight / volume[..., None] * (
                0.4 * deviator + 0.35 * (deviator - back_one) + 0.25 * (deviator - back_two)
            )
            forces.append(bond_force)
            first_states.append(back_one)
            second_states.append(back_two)
        history = jnp.stack([jnp.stack(first_states, 2), jnp.stack(second_states, 2)], 0).astype(
            jnp.bfloat16
        )
        direct_sum = jnp.zeros((3, rows, cols, points), jnp.float32)
        returned = jnp.zeros((3, rows + 2, cols + 2, points), jnp.float32)
        for index, (rs, cs) in enumerate(stencil_offsets):
            pulled = forces[index][None] * shapes[index][1]
            direct_sum = direct_sum + jnp.sum(pulled, axis=-1)
            returned = returned.at[:, 1 + rs : 1 + rs + rows, 1 + cs : 1 + cs + cols].add(
                -jnp.sum(pulled, axis=-2)
            )
        from_right = return_across(returned[:, :, 0], -1)
        from_left = return_across(returned[:, :, cols + 1], 1)
        returned = returned.at[:, :, cols].add(from_right)
        returned = returned.at[:, :, 1].add(from_left)
        from_below = return_along(returned[:, 0, 1 : cols + 1], -1)
        from_above = return_along(returned[:, rows + 1, 1 : cols + 1], 1)
        returned = returned.at[:, rows, 1 : cols + 1].add(from_below)
        returned = returned.at[:, 1, 1 : cols + 1].add(from_above)
        total_force = direct_sum + returned[:, 1 : rows + 1, 1 : cols + 1]
        velocity = velocity + 0.2 * total_force
        displacement = displacement + 0.2 * velocity
    return (displacement, velocity, history)


def solution(mesh):
    in_specs = (
        P(None, "slab", "col", None),
        P("slab", "col"),
        P(None, "slab", "col", None),
        P(None, "slab", "col", None),
        P(None, "slab", "col", None, None, None),
    )
    out_specs = (
        P(None, "slab", "col", None),
        P(None, "slab", "col", None),
        P(None, "slab", "col", None, None, None),
    )
    return jax.shard_map(
        per_device, mesh=mesh, in_specs=in_specs, out_specs=out_specs, check_vma=False
    )
```

profile of v0, /device:TPU:12, one launch (start us, length us, event | category | flops | bytes accessed | tf_op | source)
XLA Modules:
  0.0 108.8 jit_solution(6717486640619257361)
XLA Ops:
  0.6 2.8 %collective-permute-start.5 = (f32[3,1,2,128]{3,2,0,1:T(2,128)}, f32[3,1,2,128]{3,2,0,1:T(2,128)S(1)}, u32[]{:S(2)}, u32[]{:S(2)}) collective-permute-start(f32[3,1,2,128]{3,2,0,1:T(2,128)} %bitcast.1211), channel_id=1, source_target_pairs={{4,0},{8,4},{12,8},{16,12},{20,16},{24,20},{28,24},{5,1},{9,5},{13... | collective-permute-start | bytes 9224 | tf_op jit(solution)/shard_map/ppermute | solution.py:26
  3.4 1.9 %collective-permute-start.4 = (f32[3,1,2,128]{3,2,0,1:T(2,128)}, f32[3,1,2,128]{3,2,0,1:T(2,128)S(1)}, u32[]{:S(2)}, u32[]{:S(2)}) collective-permute-start(f32[3,1,2,128]{3,2,0,1:T(2,128)} %bitcast.1212), channel_id=1, source_target_pairs={{0,4},{4,8},{8,12},{12,16},{16,20},{20,24},{24,28},{1,5},{5,9},{9,... | collective-permute-start | bytes 9224 | tf_op jit(solution)/shard_map/ppermute | solution.py:25
  6.8 4.5 %collective-permute-start.1 = (f32[4,1,2,128]{3,2,0,1:T(2,128)S(1)}, f32[4,1,2,128]{3,2,0,1:T(2,128)S(1)}, u32[]{:S(2)}, u32[]{:S(2)}) collective-permute-start(f32[4,1,2,128]{3,2,0,1:T(2,128)S(1)} %pad_maximum_fusion.9), channel_id=1, source_target_pairs={{4,0},{8,4},{12,8},{16,12},{20,16},{24,20},{28,24},{5,1},{9,5},{13... | collective-permute-start | bytes 12296 | tf_op jit(solution)/shard_map/ppermute | solution.py:26
  11.3 1.9 %collective-permute-start = (f32[4,1,2,128]{3,2,0,1:T(2,128)S(1)}, f32[4,1,2,128]{3,2,0,1:T(2,128)S(1)}, u32[]{:S(2)}, u32[]{:S(2)}) collective-permute-start(f32[4,1,2,128]{3,2,0,1:T(2,128)S(1)} %pad_maximum_fusion.9), channel_id=1, source_target_pairs={{0,4},{4,8},{8,12},{12,16},{16,20},{20,24},{24,28},{1,5},{5,9},{9,... | collective-permute-start | bytes 12296 | tf_op jit(solution)/shard_map/ppermute | solution.py:25
  17.8 3.5 %collective-permute-start.2 = (f32[4,3,1,128]{3,2,0,1:T(1,128)S(1)}, f32[4,3,1,128]{3,2,0,1:T(1,128)S(1)}, u32[]{:S(2)}, u32[]{:S(2)}) collective-permute-start(f32[4,3,1,128]{3,2,0,1:T(1,128)S(1)} %get-tuple-element.563), channel_id=1, source_target_pairs={{0,1},{1,2},{2,3},{4,5},{5,6},{6,7},{8,9},{9,10},{10,11},{12,13},{... | collective-permute-start | bytes 18440 | tf_op jit(solution)/shard_map/ppermute | solution.py:25
  21.3 2.4 %collective-permute-start.3 = (f32[4,3,1,128]{3,2,0,1:T(1,128)S(1)}, f32[4,3,1,128]{3,2,0,1:T(1,128)S(1)}, u32[]{:S(2)}, u32[]{:S(2)}) collective-permute-start(f32[4,3,1,128]{3,2,0,1:T(1,128)S(1)} %get-tuple-element.564), channel_id=1, source_target_pairs={{1,0},{2,1},{3,2},{5,4},{6,5},{7,6},{9,8},{10,9},{11,10},{13,12},{... | collective-permute-start | bytes 18440 | tf_op jit(solution)/shard_map/ppermute | solution.py:26
  23.7 3.5 %collective-permute-start.6 = (f32[3,3,1,128]{3,2,0,1:T(1,128)S(1)}, f32[3,3,1,128]{3,2,0,1:T(1,128)S(1)}, u32[]{:S(2)}, u32[]{:S(2)}) collective-permute-start(f32[3,3,1,128]{3,2,0,1:T(1,128)S(1)} %get-tuple-element.567), channel_id=1, source_target_pairs={{0,1},{1,2},{2,3},{4,5},{5,6},{6,7},{8,9},{9,10},{10,11},{12,13},{... | collective-permute-start | bytes 13832 | tf_op jit(solution)/shard_map/ppermute | solution.py:25
  27.2 2.3 %collective-permute-start.7 = (f32[3,3,1,128]{3,2,0,1:T(1,128)S(1)}, f32[3,3,1,128]{3,2,0,1:T(1,128)S(1)}, u32[]{:S(2)}, u32[]{:S(2)}) collective-permute-start(f32[3,3,1,128]{3,2,0,1:T(1,128)S(1)} %get-tuple-element.568), channel_id=1, source_target_pairs={{1,0},{2,1},{3,2},{5,4},{6,5},{7,6},{9,8},{10,9},{11,10},{13,12},{... | collective-permute-start | bytes 13832 | tf_op jit(solution)/shard_map/ppermute | solution.py:26
  29.6 3.1 %collective-permute-done.7 = f32[3,3,1,128]{3,2,0,1:T(1,128)S(1)} collective-permute-done((f32[3,3,1,128]{3,2,0,1:T(1,128)S(1)}, f32[3,3,1,128]{3,2,0,1:T(1,128)S(1)}, u32[]{:S(2)}, u32[]{:S(2)}) %collective-permute-start.7) | collective-permute-done | bytes 4640 | tf_op jit(solution)/shard_map/ppermute | solution.py:26
  34.9 2.0 %fusion.4 = (f32[2,128,128]{2,1,0:T(8,128)S(1)}, f32[2,128,128]{2,1,0:T(8,128)S(1)}, f32[2,128,128]{2,1,0:T(8,128)S(1)}, f32[2,128,128]{2,1,0:T(8,128)S(1)}, f32...) fusion(f32[3,2,128]{2,1,0:T(2,128)S(1)} %get-tuple-element.561,, ...), kind=kLoop, calls=%fused_computation.41 | loop fusion | flops 4718592 | bytes 2414592 | tf_op jit(solution)/shard_map/reduce_sum | solution.py:57
  43.1 1.9 %constant_dynamic-update-slice_fusion.50 = f32[3,3,4,128]{3,0,1,2:T(4,128)S(1)} fusion(f32[3,3,4,128]{3,0,1,2:T(4,128)S(1)} %constant_dynamic-update-slice_fusion.51, s32[]{:T(128)} %bitcast.55, s32[]{:T(128)} %bitcast.56, f32[3,2,128]{2,1,0:T(2,128)S(1)} %get-tuple-element.405, pred[]{:T(512)} %and_reduce_fusion), kind=kLoop, calls=%fused_computation.646 | loop fusion | flops 2304 | bytes 11273 | tf_op jit(solution)/shard_map/scatter-add | solution.py:121
  45.2 2.3 %collective-permute-start.8 = (f32[3,3,128]{2,0,1:T(4,128)S(1)}, f32[3,3,128]{2,0,1:T(4,128)S(1)}, u32[]{:S(2)}, u32[]{:S(2)}) collective-permute-start(f32[3,3,128]{2,0,1:T(4,128)S(1)} %slice_bitcast_fusion.3), channel_id=1, source_target_pairs={{1,0},{2,1},{3,2},{5,4},{6,5},{7,6},{9,8},{10,9},{11,10},{13,12},{... | collective-permute-start | bytes 13832 | tf_op jit(solution)/shard_map/ppermute | solution.py:15
  48.2 2.5 %collective-permute-done.8 = f32[3,3,128]{2,0,1:T(4,128)S(1)} collective-permute-done((f32[3,3,128]{2,0,1:T(4,128)S(1)}, f32[3,3,128]{2,0,1:T(4,128)S(1)}, u32[]{:S(2)}, u32[]{:S(2)}) %collective-permute-start.8) | collective-permute-done | bytes 4640 | tf_op jit(solution)/shard_map/ppermute | solution.py:15
  50.7 3.5 %collective-permute-start.9 = (f32[3,3,128]{2,0,1:T(4,128)S(1)}, f32[3,3,128]{2,0,1:T(4,128)S(1)}, u32[]{:S(2)}, u32[]{:S(2)}) collective-permute-start(f32[3,3,128]{2,0,1:T(4,128)S(1)} %get-tuple-element.535), channel_id=1, source_target_pairs={{0,1},{1,2},{2,3},{4,5},{5,6},{6,7},{8,9},{9,10},{10,11},{12,13},{... | collective-permute-start | bytes 13832 | tf_op jit(solution)/shard_map/ppermute | solution.py:15
  54.3 1.9 %collective-permute-done.9 = f32[3,3,128]{2,0,1:T(4,128)S(1)} collective-permute-done((f32[3,3,128]{2,0,1:T(4,128)S(1)}, f32[3,3,128]{2,0,1:T(4,128)S(1)}, u32[]{:S(2)}, u32[]{:S(2)}) %collective-permute-start.9) | collective-permute-done | bytes 4640 | tf_op jit(solution)/shard_map/ppermute | solution.py:15
  56.2 1.9 %collective-permute-start.10 = (f32[3,2,128]{2,0,1:T(4,128)S(1)}, f32[3,2,128]{2,0,1:T(4,128)S(1)}, u32[]{:S(2)}, u32[]{:S(2)}) collective-permute-start(f32[3,2,128]{2,0,1:T(4,128)S(1)} %get-tuple-element.533), channel_id=1, source_target_pairs={{4,0},{8,4},{12,8},{16,12},{20,16},{24,20},{28,24},{5,1},{9,5},{13... | collective-permute-start | bytes 9224 | tf_op jit(solution)/shard_map/ppermute | solution.py:15
  58.1 2.4 %collective-permute-start.11 = (f32[3,2,128]{2,0,1:T(4,128)S(1)}, f32[3,2,128]{2,0,1:T(4,128)S(1)}, u32[]{:S(2)}, u32[]{:S(2)}) collective-permute-start(f32[3,2,128]{2,0,1:T(4,128)S(1)} %get-tuple-element.534), channel_id=1, source_target_pairs={{0,4},{4,8},{8,12},{12,16},{16,20},{20,24},{24,28},{1,5},{5,9},{9,... | collective-permute-start | bytes 9224 | tf_op jit(solution)/shard_map/ppermute | solution.py:15
  60.7 3.2 %collective-permute-done.11 = f32[3,2,128]{2,0,1:T(4,128)S(1)} collective-permute-done((f32[3,2,128]{2,0,1:T(4,128)S(1)}, f32[3,2,128]{2,0,1:T(4,128)S(1)}, u32[]{:S(2)}, u32[]{:S(2)}) %collective-permute-start.11) | collective-permute-done | bytes 3104 | tf_op jit(solution)/shard_map/ppermute | solution.py:15
  64.0 1.9 %collective-permute-start.13 = (f32[3,1,2,128]{3,2,0,1:T(2,128)S(1)}, f32[3,1,2,128]{3,2,0,1:T(2,128)S(1)}, u32[]{:S(2)}, u32[]{:S(2)}) collective-permute-start(f32[3,1,2,128]{3,2,0,1:T(2,128)S(1)} %get-tuple-element.454), channel_id=1, source_target_pairs={{4,0},{8,4},{12,8},{16,12},{20,16},{24,20},{28,24},{5,1},{9,5},{13... | collective-permute-start | bytes 9224 | tf_op jit(solution)/shard_map/ppermute | solution.py:26
  65.9 2.4 %collective-permute-start.12 = (f32[3,1,2,128]{3,2,0,1:T(2,128)S(1)}, f32[3,1,2,128]{3,2,0,1:T(2,128)S(1)}, u32[]{:S(2)}, u32[]{:S(2)}) collective-permute-start(f32[3,1,2,128]{3,2,0,1:T(2,128)S(1)} %get-tuple-element.454), channel_id=1, source_target_pairs={{0,4},{4,8},{8,12},{12,16},{16,20},{20,24},{24,28},{1,5},{5,9},{9,... | collective-permute-start | bytes 9224 | tf_op jit(solution)/shard_map/ppermute | solution.py:25
  68.5 3.2 %collective-permute-done.12 = f32[3,1,2,128]{3,2,0,1:T(2,128)S(1)} collective-permute-done((f32[3,1,2,128]{3,2,0,1:T(2,128)S(1)}, f32[3,1,2,128]{3,2,0,1:T(2,128)S(1)}, u32[]{:S(2)}, u32[]{:S(2)}) %collective-permute-start.12) | collective-permute-done | bytes 3104 | tf_op jit(solution)/shard_map/ppermute | solution.py:25
  71.8 3.5 %collective-permute-start.14 = (f32[3,3,1,128]{3,2,0,1:T(1,128)S(1)}, f32[3,3,1,128]{3,2,0,1:T(1,128)S(1)}, u32[]{:S(2)}, u32[]{:S(2)}) collective-permute-start(f32[3,3,1,128]{3,2,0,1:T(1,128)S(1)} %get-tuple-element.565), channel_id=1, source_target_pairs={{0,1},{1,2},{2,3},{4,5},{5,6},{6,7},{8,9},{9,10},{10,11},{12,13},{... | collective-permute-start | bytes 13832 | tf_op jit(solution)/shard_map/ppermute | solution.py:25
  75.2 2.5 %collective-permute-start.15 = (f32[3,3,1,128]{3,2,0,1:T(1,128)S(1)}, f32[3,3,1,128]{3,2,0,1:T(1,128)S(1)}, u32[]{:S(2)}, u32[]{:S(2)}) collective-permute-start(f32[3,3,1,128]{3,2,0,1:T(1,128)S(1)} %get-tuple-element.566), channel_id=1, source_target_pairs={{1,0},{2,1},{3,2},{5,4},{6,5},{7,6},{9,8},{10,9},{11,10},{13,12},{... | collective-permute-start | bytes 13832 | tf_op jit(solution)/shard_map/ppermute | solution.py:26
  78.0 2.8 %collective-permute-done.15 = f32[3,3,1,128]{3,2,0,1:T(1,128)S(1)} collective-permute-done((f32[3,3,1,128]{3,2,0,1:T(1,128)S(1)}, f32[3,3,1,128]{3,2,0,1:T(1,128)S(1)}, u32[]{:S(2)}, u32[]{:S(2)}) %collective-permute-start.15) | collective-permute-done | bytes 4640 | tf_op jit(solution)/shard_map/ppermute | solution.py:26
  87.3 1.9 %constant_dynamic-update-slice_fusion.42 = f32[3,3,4,128]{3,0,1,2:T(4,128)S(1)} fusion(f32[3,3,4,128]{3,0,1,2:T(4,128)S(1)} %constant_dynamic-update-slice_fusion.43, s32[]{:T(128)} %bitcast.55, s32[]{:T(128)} %bitcast.56, f32[3,2,128]{2,1,0:T(2,128)S(1)} %get-tuple-element.382, pred[]{:T(512)} %and_reduce_fusion), kind=kLoop, calls=%fused_computation.637 | loop fusion | flops 2304 | bytes 11273 | tf_op jit(solution)/shard_map/scatter-add | solution.py:121
  89.4 2.4 %collective-permute-start.16 = (f32[3,3,128]{2,0,1:T(4,128)S(1)}, f32[3,3,128]{2,0,1:T(4,128)S(1)}, u32[]{:S(2)}, u32[]{:S(2)}) collective-permute-start(f32[3,3,128]{2,0,1:T(4,128)S(1)} %slice_bitcast_fusion.1), channel_id=1, source_target_pairs={{1,0},{2,1},{3,2},{5,4},{6,5},{7,6},{9,8},{10,9},{11,10},{13,12},{... | collective-permute-start | bytes 13832 | tf_op jit(solution)/shard_map/ppermute | solution.py:15
  92.9 2.0 %collective-permute-done.16 = f32[3,3,128]{2,0,1:T(4,128)S(1)} collective-permute-done((f32[3,3,128]{2,0,1:T(4,128)S(1)}, f32[3,3,128]{2,0,1:T(4,128)S(1)}, u32[]{:S(2)}, u32[]{:S(2)}) %collective-permute-start.16) | collective-permute-done | bytes 4640 | tf_op jit(solution)/shard_map/ppermute | solution.py:15
  94.9 1.9 %collective-permute-start.17 = (f32[3,3,128]{2,0,1:T(4,128)S(1)}, f32[3,3,128]{2,0,1:T(4,128)S(1)}, u32[]{:S(2)}, u32[]{:S(2)}) collective-permute-start(f32[3,3,128]{2,0,1:T(4,128)S(1)} %get-tuple-element.531), channel_id=1, source_target_pairs={{0,1},{1,2},{2,3},{4,5},{5,6},{6,7},{8,9},{9,10},{10,11},{12,13},{... | collective-permute-start | bytes 13832 | tf_op jit(solution)/shard_map/ppermute | solution.py:15
  97.0 3.4 %collective-permute-done.17 = f32[3,3,128]{2,0,1:T(4,128)S(1)} collective-permute-done((f32[3,3,128]{2,0,1:T(4,128)S(1)}, f32[3,3,128]{2,0,1:T(4,128)S(1)}, u32[]{:S(2)}, u32[]{:S(2)}) %collective-permute-start.17) | collective-permute-done | bytes 4640 | tf_op jit(solution)/shard_map/ppermute | solution.py:15
  100.5 1.9 %collective-permute-start.18 = (f32[3,2,128]{2,1,0:T(2,128)S(1)}, f32[3,2,128]{2,1,0:T(2,128)S(1)}, u32[]{:S(2)}, u32[]{:S(2)}) collective-permute-start(f32[3,2,128]{2,1,0:T(2,128)S(1)} %get-tuple-element.537), channel_id=1, source_target_pairs={{4,0},{8,4},{12,8},{16,12},{20,16},{24,20},{28,24},{5,1},{9,5},{13... | collective-permute-start | bytes 9224 | tf_op jit(solution)/shard_map/ppermute | solution.py:15
  102.4 2.4 %collective-permute-start.19 = (f32[3,2,128]{2,1,0:T(2,128)S(1)}, f32[3,2,128]{2,1,0:T(2,128)S(1)}, u32[]{:S(2)}, u32[]{:S(2)}) collective-permute-start(f32[3,2,128]{2,1,0:T(2,128)S(1)} %get-tuple-element.538), channel_id=1, source_target_pairs={{0,4},{4,8},{8,12},{12,16},{16,20},{20,24},{24,28},{1,5},{5,9},{9,... | collective-permute-start | bytes 9224 | tf_op jit(solution)/shard_map/ppermute | solution.py:15
  106.1 2.1 %collective-permute-done.19 = f32[3,2,128]{2,1,0:T(2,128)S(1)} collective-permute-done((f32[3,2,128]{2,1,0:T(2,128)S(1)}, f32[3,2,128]{2,1,0:T(2,128)S(1)}, u32[]{:S(2)}, u32[]{:S(2)}) %collective-permute-start.19) | collective-permute-done | bytes 3104 | tf_op jit(solution)/shard_map/ppermute | solution.py:15
  (110 shorter events, 25.7 us)
Async XLA Ops:
  0.6 15.2 %collective-permute-start.5 = (f32[3,1,2,128]{3,2,0,1:T(2,128)}, f32[3,1,2,128]{3,2,0,1:T(2,128)S(1)}, u32[]{:S(2)}, u32[]{:S(2)}) collective-permute-start(f32[3,1,2,128]{3,2,0,1:T(2,128)} %bitcast.1211), channel_id=1, source_target_pairs={{4,0},{8,4},{12,8},{16,12},{20,16},{24,20},{28,24},{5,1},{9,5},{13... | collective-permute-start | bytes 9224 | tf_op jit(solution)/shard_map/ppermute | solution.py:26
  3.4 12.4 %collective-permute-start.4 = (f32[3,1,2,128]{3,2,0,1:T(2,128)}, f32[3,1,2,128]{3,2,0,1:T(2,128)S(1)}, u32[]{:S(2)}, u32[]{:S(2)}) collective-permute-start(f32[3,1,2,128]{3,2,0,1:T(2,128)} %bitcast.1212), channel_id=1, source_target_pairs={{0,4},{4,8},{8,12},{12,16},{16,20},{20,24},{24,28},{1,5},{5,9},{9,... | collective-permute-start | bytes 9224 | tf_op jit(solution)/shard_map/ppermute | solution.py:25
  6.8 9.7 %collective-permute-start.1 = (f32[4,1,2,128]{3,2,0,1:T(2,128)S(1)}, f32[4,1,2,128]{3,2,0,1:T(2,128)S(1)}, u32[]{:S(2)}, u32[]{:S(2)}) collective-permute-start(f32[4,1,2,128]{3,2,0,1:T(2,128)S(1)} %pad_maximum_fusion.9), channel_id=1, source_target_pairs={{4,0},{8,4},{12,8},{16,12},{20,16},{24,20},{28,24},{5,1},{9,5},{13... | collective-permute-start | bytes 12296 | tf_op jit(solution)/shard_map/ppermute | solution.py:26
  11.3 5.8 %collective-permute-start = (f32[4,1,2,128]{3,2,0,1:T(2,128)S(1)}, f32[4,1,2,128]{3,2,0,1:T(2,128)S(1)}, u32[]{:S(2)}, u32[]{:S(2)}) collective-permute-start(f32[4,1,2,128]{3,2,0,1:T(2,128)S(1)} %pad_maximum_fusion.9), channel_id=1, source_target_pairs={{0,4},{4,8},{8,12},{12,16},{16,20},{20,24},{24,28},{1,5},{5,9},{9,... | collective-permute-start | bytes 12296 | tf_op jit(solution)/shard_map/ppermute | solution.py:25
  17.8 11.7 %collective-permute-start.2 = (f32[4,3,1,128]{3,2,0,1:T(1,128)S(1)}, f32[4,3,1,128]{3,2,0,1:T(1,128)S(1)}, u32[]{:S(2)}, u32[]{:S(2)}) collective-permute-start(f32[4,3,1,128]{3,2,0,1:T(1,128)S(1)} %get-tuple-element.563), channel_id=1, source_target_pairs={{0,1},{1,2},{2,3},{4,5},{5,6},{6,7},{8,9},{9,10},{10,11},{12,13},{... | collective-permute-start | bytes 18440 | tf_op jit(solution)/shard_map/ppermute | solution.py:25
  21.3 8.2 %collective-permute-start.3 = (f32[4,3,1,128]{3,2,0,1:T(1,128)S(1)}, f32[4,3,1,128]{3,2,0,1:T(1,128)S(1)}, u32[]{:S(2)}, u32[]{:S(2)}) collective-permute-start(f32[4,3,1,128]{3,2,0,1:T(1,128)S(1)} %get-tuple-element.564), channel_id=1, source_target_pairs={{1,0},{2,1},{3,2},{5,4},{6,5},{7,6},{9,8},{10,9},{11,10},{13,12},{... | collective-permute-start | bytes 18440 | tf_op jit(solution)/shard_map/ppermute | solution.py:26
  23.7 5.9 %collective-permute-start.6 = (f32[3,3,1,128]{3,2,0,1:T(1,128)S(1)}, f32[3,3,1,128]{3,2,0,1:T(1,128)S(1)}, u32[]{:S(2)}, u32[]{:S(2)}) collective-permute-start(f32[3,3,1,128]{3,2,0,1:T(1,128)S(1)} %get-tuple-element.567), channel_id=1, source_target_pairs={{0,1},{1,2},{2,3},{4,5},{5,6},{6,7},{8,9},{9,10},{10,11},{12,13},{... | collective-permute-start | bytes 13832 | tf_op jit(solution)/shard_map/ppermute | solution.py:25
  27.2 5.5 %collective-permute-start.7 = (f32[3,3,1,128]{3,2,0,1:T(1,128)S(1)}, f32[3,3,1,128]{3,2,0,1:T(1,128)S(1)}, u32[]{:S(2)}, u32[]{:S(2)}) collective-permute-start(f32[3,3,1,128]{3,2,0,1:T(1,128)S(1)} %get-tuple-element.568), channel_id=1, source_target_pairs={{1,0},{2,1},{3,2},{5,4},{6,5},{7,6},{9,8},{10,9},{11,10},{13,12},{... | collective-permute-start | bytes 13832 | tf_op jit(solution)/shard_map/ppermute | solution.py:26
  36.8 1.3 %copy-start = (bf16[2,1,2,9,128,128]{5,4,3,2,1,0:T(8,128)(2,1)S(1)}, bf16[2,1,2,9,128,128]{5,4,3,2,1,0:T(8,128)(2,1)}, u32[]{:S(2)}) copy-start(bf16[2,1,2,9,128,128]{5,4,3,2,1,0:T(8,128)(2,1)} %param.61) | copy-start | bytes 3538948
  45.2 5.5 %collective-permute-start.8 = (f32[3,3,128]{2,0,1:T(4,128)S(1)}, f32[3,3,128]{2,0,1:T(4,128)S(1)}, u32[]{:S(2)}, u32[]{:S(2)}) collective-permute-start(f32[3,3,128]{2,0,1:T(4,128)S(1)} %slice_bitcast_fusion.3), channel_id=1, source_target_pairs={{1,0},{2,1},{3,2},{5,4},{6,5},{7,6},{9,8},{10,9},{11,10},{13,12},{... | collective-permute-start | bytes 13832 | tf_op jit(solution)/shard_map/ppermute | solution.py:15
  47.8 16.1 %copy-start.2 = (f32[3,1,2,128]{3,2,1,0:T(2,128)S(1)}, f32[3,1,2,128]{3,2,1,0:T(2,128)}, u32[]{:S(2)}) copy-start(f32[3,1,2,128]{3,2,1,0:T(2,128)} %param.59) | copy-start | bytes 9220
  47.8 16.1 %copy-start.3 = (f32[3,1,2,128]{3,2,1,0:T(2,128)S(1)}, f32[3,1,2,128]{3,2,1,0:T(2,128)}, u32[]{:S(2)}) copy-start(f32[3,1,2,128]{3,2,1,0:T(2,128)} %param.60) | copy-start | bytes 9220
  48.2 32.6 %copy-start.1 = (f32[3,1,2,128]{3,2,1,0:T(2,128)S(1)}, f32[3,1,2,128]{3,2,1,0:T(2,128)}, u32[]{:S(2)}) copy-start(f32[3,1,2,128]{3,2,1,0:T(2,128)} %param.57) | copy-start | bytes 9220
  50.7 5.5 %collective-permute-start.9 = (f32[3,3,128]{2,0,1:T(4,128)S(1)}, f32[3,3,128]{2,0,1:T(4,128)S(1)}, u32[]{:S(2)}, u32[]{:S(2)}) collective-permute-start(f32[3,3,128]{2,0,1:T(4,128)S(1)} %get-tuple-element.535), channel_id=1, source_target_pairs={{0,1},{1,2},{2,3},{4,5},{5,6},{6,7},{8,9},{9,10},{10,11},{12,13},{... | collective-permute-start | bytes 13832 | tf_op jit(solution)/shard_map/ppermute | solution.py:15
  56.2 4.5 %collective-permute-start.10 = (f32[3,2,128]{2,0,1:T(4,128)S(1)}, f32[3,2,128]{2,0,1:T(4,128)S(1)}, u32[]{:S(2)}, u32[]{:S(2)}) collective-permute-start(f32[3,2,128]{2,0,1:T(4,128)S(1)} %get-tuple-element.533), channel_id=1, source_target_pairs={{4,0},{8,4},{12,8},{16,12},{20,16},{24,20},{28,24},{5,1},{9,5},{13... | collective-permute-start | bytes 9224 | tf_op jit(solution)/shard_map/ppermute | solution.py:15
  58.1 5.8 %collective-permute-start.11 = (f32[3,2,128]{2,0,1:T(4,128)S(1)}, f32[3,2,128]{2,0,1:T(4,128)S(1)}, u32[]{:S(2)}, u32[]{:S(2)}) collective-permute-start(f32[3,2,128]{2,0,1:T(4,128)S(1)} %get-tuple-element.534), channel_id=1, source_target_pairs={{0,4},{4,8},{8,12},{12,16},{16,20},{20,24},{24,28},{1,5},{5,9},{9,... | collective-permute-start | bytes 9224 | tf_op jit(solution)/shard_map/ppermute | solution.py:15
  64.0 4.5 %collective-permute-start.13 = (f32[3,1,2,128]{3,2,0,1:T(2,128)S(1)}, f32[3,1,2,128]{3,2,0,1:T(2,128)S(1)}, u32[]{:S(2)}, u32[]{:S(2)}) collective-permute-start(f32[3,1,2,128]{3,2,0,1:T(2,128)S(1)} %get-tuple-element.454), channel_id=1, source_target_pairs={{4,0},{8,4},{12,8},{16,12},{20,16},{24,20},{28,24},{5,1},{9,5},{13... | collective-permute-start | bytes 9224 | tf_op jit(solution)/shard_map/ppermute | solution.py:26
  65.9 5.8 %collective-permute-start.12 = (f32[3,1,2,128]{3,2,0,1:T(2,128)S(1)}, f32[3,1,2,128]{3,2,0,1:T(2,128)S(1)}, u32[]{:S(2)}, u32[]{:S(2)}) collective-permute-start(f32[3,1,2,128]{3,2,0,1:T(2,128)S(1)} %get-tuple-element.454), channel_id=1, source_target_pairs={{0,4},{4,8},{8,12},{12,16},{16,20},{20,24},{24,28},{1,5},{5,9},{9,... | collective-permute-start | bytes 9224 | tf_op jit(solution)/shard_map/ppermute | solution.py:25
  71.8 6.2 %collective-permute-start.14 = (f32[3,3,1,128]{3,2,0,1:T(1,128)S(1)}, f32[3,3,1,128]{3,2,0,1:T(1,128)S(1)}, u32[]{:S(2)}, u32[]{:S(2)}) collective-permute-start(f32[3,3,1,128]{3,2,0,1:T(1,128)S(1)} %get-tuple-element.565), channel_id=1, source_target_pairs={{0,1},{1,2},{2,3},{4,5},{5,6},{6,7},{8,9},{9,10},{10,11},{12,13},{... | collective-permute-start | bytes 13832 | tf_op jit(solution)/shard_map/ppermute | solution.py:25
  75.2 5.5 %collective-permute-start.15 = (f32[3,3,1,128]{3,2,0,1:T(1,128)S(1)}, f32[3,3,1,128]{3,2,0,1:T(1,128)S(1)}, u32[]{:S(2)}, u32[]{:S(2)}) collective-permute-start(f32[3,3,1,128]{3,2,0,1:T(1,128)S(1)} %get-tuple-element.566), channel_id=1, source_target_pairs={{1,0},{2,1},{3,2},{5,4},{6,5},{7,6},{9,8},{10,9},{11,10},{13,12},{... | collective-permute-start | bytes 13832 | tf_op jit(solution)/shard_map/ppermute | solution.py:26
  89.4 5.5 %collective-permute-start.16 = (f32[3,3,128]{2,0,1:T(4,128)S(1)}, f32[3,3,128]{2,0,1:T(4,128)S(1)}, u32[]{:S(2)}, u32[]{:S(2)}) collective-permute-start(f32[3,3,128]{2,0,1:T(4,128)S(1)} %slice_bitcast_fusion.1), channel_id=1, source_target_pairs={{1,0},{2,1},{3,2},{5,4},{6,5},{7,6},{9,8},{10,9},{11,10},{13,12},{... | collective-permute-start | bytes 13832 | tf_op jit(solution)/shard_map/ppermute | solution.py:15
  94.9 5.5 %collective-permute-start.17 = (f32[3,3,128]{2,0,1:T(4,128)S(1)}, f32[3,3,128]{2,0,1:T(4,128)S(1)}, u32[]{:S(2)}, u32[]{:S(2)}) collective-permute-start(f32[3,3,128]{2,0,1:T(4,128)S(1)} %get-tuple-element.531), channel_id=1, source_target_pairs={{0,1},{1,2},{2,3},{4,5},{5,6},{6,7},{8,9},{9,10},{10,11},{12,13},{... | collective-permute-start | bytes 13832 | tf_op jit(solution)/shard_map/ppermute | solution.py:15
  100.5 5.6 %collective-permute-start.18 = (f32[3,2,128]{2,1,0:T(2,128)S(1)}, f32[3,2,128]{2,1,0:T(2,128)S(1)}, u32[]{:S(2)}, u32[]{:S(2)}) collective-permute-start(f32[3,2,128]{2,1,0:T(2,128)S(1)} %get-tuple-element.537), channel_id=1, source_target_pairs={{4,0},{8,4},{12,8},{16,12},{20,16},{24,20},{28,24},{5,1},{9,5},{13... | collective-permute-start | bytes 9224 | tf_op jit(solution)/shard_map/ppermute | solution.py:15
  102.4 5.8 %collective-permute-start.19 = (f32[3,2,128]{2,1,0:T(2,128)S(1)}, f32[3,2,128]{2,1,0:T(2,128)S(1)}, u32[]{:S(2)}, u32[]{:S(2)}) collective-permute-start(f32[3,2,128]{2,1,0:T(2,128)S(1)} %get-tuple-element.538), channel_id=1, source_target_pairs={{0,4},{4,8},{8,12},{12,16},{16,20},{20,24},{24,28},{1,5},{5,9},{9,... | collective-permute-start | bytes 9224 | tf_op jit(solution)/shard_map/ppermute | solution.py:15
where the time goes:
time: 110 us; the launch traced here: 109 us
  starting transfers between devices  51.9 us (47%)
  other arithmetic  28.3 us (26%)
  waiting for transfers between devices  24.9 us (23%)
  local copies, waits for them, and re-layouts  2.49 us (2%)
  between operations  1.19 us (1%)
    ppermute x8, starting transfers between devices, passed_along(): lax.ppermute(value, axis, [(source, source + steps) for source in range(l...  18.7 us
    ppermute x6, starting transfers between devices, with_halo(): before = lax.ppermute(last, axis, up)  16.7 us
    ppermute x6, starting transfers between devices, with_halo(): after = lax.ppermute(leading, axis, down)  16.5 us
    ppermute x8, waiting for transfers between devices, passed_along(): lax.ppermute(value, axis, [(source, source + steps) for source in range(l...  15.2 us
    scatter-add x16, other arithmetic, per_device(): returned.at[:, 1 + rs:1 + rs + rows, 1 + cs:1 + cs + cols]  6.59 us
    ppermute x6, waiting for transfers between devices, with_halo(): after = lax.ppermute(leading, axis, down)  5.88 us
    ppermute x6, waiting for transfers between devices, with_halo(): before = lax.ppermute(last, axis, up)  3.85 us
    add x6, other arithmetic, per_device(): bond_force + 7.5 * weight / volume[..., None] * (0.4 * deviator + 0.35 *...  3.83 us
  transfers between devices with their start and end apart: 20, of which 10 were waited for; matrix products, arithmetic and copies ran while one was open for 8% of the time, Pallas kernels for 0%

commit v1 on v0

v1 whole, which is shorter than its diff:
```python
import functools

import jax
import jax.numpy as jnp
from jax import lax
from jax.experimental import pallas as pl
from jax.experimental.pallas import tpu as pltpu
from jax.sharding import PartitionSpec as P

MESH = pl.DeviceIdType.MESH
STENCIL = [(-1, -1), (-1, 0), (-1, 1), (0, -1), (0, 0), (0, 1), (1, -1), (1, 0), (1, 1)]
NEAR = [(dr, dc) for dr in (-1, 0, 1) for dc in (-1, 0, 1) if (dr, dc) != (0, 0)]
WIDE = [(dr, dc) for dr in (-2, -1, 0, 1, 2) for dc in (-1, 0, 1) if (dr, dc) != (0, 0)]
CHUNK = 16
TINY = 1e-30


def kernel(
    slabs, sections, tiles, points,
    rest_ref, fill_ref, disp_ref, vel_ref, hist_hbm,
    disp_out, vel_out, hist_out,
    hist, halo, place, pulls, last_pulls, wide_in, near_in,
    length_s, weight_s, stretch_s, pull_s,
    home_rest, home_place, sums, theta, inverse_mass, partial,
    hist_in_sem, hist_out_sem, send_a, recv_a, send_b, recv_b, send_c, recv_c,
):
    r, c = lax.axis_index("slab"), lax.axis_index("col")
    chunks = points // CHUNK
    f32 = jnp.float32

    def inside(dr, dc):
        row, col = r + dr, c + dc
        return (row >= 0) & (row < slabs) & (col >= 0) & (col < sections)

    load_hist = pltpu.make_async_copy(hist_hbm, hist, hist_in_sem)
    load_hist.start()

    halo[...] = jnp.zeros_like(halo)
    wide_in[...] = jnp.zeros_like(wide_in)
    near_in[...] = jnp.zeros_like(near_in)

    barrier = pltpu.get_barrier_semaphore()
    for dr, dc in WIDE:
        @pl.when(inside(dr, dc))
        def _():
            pl.semaphore_signal(barrier, inc=1, device_id=(r + dr, c + dc), device_id_type=MESH)

    lane = lax.broadcasted_iota(jnp.int32, (1, points), 1)
    for t in range(tiles):
        for i in range(3):
            halo[1, 1 + t, i : i + 1, :] = rest_ref[i, 0, t : t + 1, :]
            halo[1, 1 + t, 4 + i : 5 + i, :] = disp_ref[i, 0, t : t + 1, :]
            halo[1, 1 + t, 8 + i : 9 + i, :] = vel_ref[i, 0, t : t + 1, :]
        halo[1, 1 + t, 3:4, :] = (lane < fill_ref[0:1, t : t + 1]).astype(f32)

    low_rows = jnp.minimum(r, 2)
    high_rows = jnp.minimum(slabs - 1 - r, 2)
    side_cols = jnp.minimum(c, 1) + jnp.minimum(sections - 1 - c, 1)
    pl.semaphore_wait(barrier, (low_rows + high_rows + 1) * (side_cols + 1) - 1)

    def halo_copy(n):
        dr, dc = NEAR[n]
        src, dst, count = {0: (1, 1, tiles), 1: (tiles, 0, 1), -1: (1, tiles + 1, 1)}[dc]
        return pltpu.make_async_remote_copy(
            src_ref=halo.at[1, pl.ds(src, count)],
            dst_ref=halo.at[1 - dr, pl.ds(dst, count)],
            send_sem=send_a.at[n], recv_sem=recv_a.at[n],
            device_id=(r + dr, c + dc), device_id_type=MESH,
        )

    def wide_copy(n):
        dr, dc = WIDE[n]
        row, rows = max(0, dr), min(2, 2 + dr) - max(0, dr) + 1
        col = max(0, tiles * dc)
        cols = min(tiles + 1, tiles + 1 + tiles * dc) - col + 1
        return pltpu.make_async_remote_copy(
            src_ref=pulls.at[pl.ds(row, rows), pl.ds(col, cols)],
            dst_ref=wide_in.at[n, pl.ds(row - dr, rows), pl.ds(col - tiles * dc, cols)],
            send_sem=send_b.at[n], recv_sem=recv_b.at[n],
            device_id=(r + dr, c + dc), device_id_type=MESH,
        )

    def near_copy(n):
        dr, dc = NEAR[n]
        src, dst, count = {0: (1, 0, tiles), 1: (tiles + 1, 0, 1), -1: (0, tiles - 1, 1)}[dc]
        return pltpu.make_async_remote_copy(
            src_ref=last_pulls.at[1 + dr, pl.ds(src, count)],
            dst_ref=near_in.at[n, pl.ds(dst, count)],
            send_sem=send_c.at[n], recv_sem=recv_c.at[n],
            device_id=(r + dr, c + dc), device_id_type=MESH,
        )

    def start_all(peers, copy):
        for n, (dr, dc) in enumerate(peers):
            @pl.when(inside(dr, dc))
            def _():
                copy(n).start()

    def receive_all(peers, copy):
        for n, (dr, dc) in enumerate(peers):
            @pl.when(inside(-dr, -dc))
            def _():
                copy(n).wait_recv()

    def sent_all(peers, copy):
        for n, (dr, dc) in enumerate(peers):
            @pl.when(inside(dr, dc))
            def _():
                copy(n).wait_send()

    def over_lanes(rows):
        turned = rows.T
        return [jnp.broadcast_to(turned[:, i : i + 1], (points, points)) for i in range(3)]

    start_all(NEAR, halo_copy)
    for t in range(tiles):
        own = halo[1, 1 + t, 0:8, :]
        for i, wide in enumerate(over_lanes(own)):
            home_rest[t, i] = wide
        for i, wide in enumerate(over_lanes(own + pltpu.roll(own, 4, 0))):
            home_place[t, i] = wide
    receive_all(NEAR, halo_copy)
    place[...] = halo[:, :, 0:4, :] + halo[:, :, 4:8, :]

    def measure(first):
        for t in range(tiles):
            def body(n, carry):
                start = pl.multiple_of(n * CHUNK, CHUNK)
                at = pl.ds(start, CHUNK)
                volume = jnp.zeros((CHUNK, points), f32)
                spread = jnp.zeros((CHUNK, points), f32)
                for k, (dr, dc) in enumerate(STENCIL):
                    far = (1 + dr, 1 + t + dc)
                    if first:
                        bond = [halo[far[0], far[1], i : i + 1, :] - home_rest[t, i, at, :] for i in range(3)]
                        square = bond[0] * bond[0] + bond[1] * bond[1] + bond[2] * bond[2]
                        length = square * lax.rsqrt(jnp.maximum(square, TINY))
                        close = jnp.maximum(1.0 - length, 0.0)
                        weight = close * close * halo[far[0], far[1], 3:4, :]
                        if (dr, dc) == (0, 0):
                            a = lax.broadcasted_iota(jnp.int32, (CHUNK, points), 0) + start
                            b = lax.broadcasted_iota(jnp.int32, (CHUNK, points), 1)
                            weight = jnp.where(a == b, 0.0, weight)
                        length_s[t, k, at, :] = length
                        weight_s[t, k, at, :] = weight
                    else:
                        length = length_s[t, k, at, :]
                        weight = weight_s[t, k, at, :]
                    reach = weight * length
                    if first:
                        volume = volume + reach * length
                    apart = [place[far[0], far[1], i : i + 1, :] - home_place[t, i, at, :] for i in range(3)]
                    square = apart[0] * apart[0] + apart[1] * apart[1] + apart[2] * apart[2]
                    stretch = square * lax.rsqrt(jnp.maximum(square, TINY)) - length
                    stretch_s[t, k, at, :] = stretch
                    pull_s[t, k, at, :] = weight * lax.rsqrt(square + 0.01)
                    spread = spread + reach * stretch
                sums[0, t, at, :] = spread
                if first:
                    sums[1, t, at, :] = volume
                return carry
            lax.fori_loop(0, chunks, body, 0)
        for t in range(tiles):
            if first:
                volume = jnp.sum(sums[1, t], axis=-1, keepdims=True)
                a = lax.broadcasted_iota(jnp.int32, (points, 1), 0)
                inverse = jnp.where(a < fill_ref[0:1, t : t + 1], 1.0 / jnp.maximum(volume, 1.0), 0.0)
                inverse_mass[t] = jnp.broadcast_to(inverse, (points, points))
            spread = jnp.sum(sums[0, t], axis=-1, keepdims=True)
            theta[t] = jnp.broadcast_to(spread, (points, points)) * inverse_mass[t]

    def pull(result):
        for t in range(tiles):
            def body(n, carry):
                at = pl.ds(pl.multiple_of(n * CHUNK, CHUNK), CHUNK)
                scaled = theta[t, at, :] * 2.64375
                inverse = inverse_mass[t, at, :]
                direct = [jnp.zeros((CHUNK, points), f32)] * 3
                for k, (dr, dc) in enumerate(STENCIL):
                    one = hist[0, 0, t, k, at, :].astype(f32)
                    two = hist[1, 0, t, k, at, :].astype(f32)
                    force = scaled * length_s[t, k, at, :] + 6.35625 * stretch_s[t, k, at, :]
                    force = force - 1.575 * one - 1.78125 * two
                    force = force * inverse * pull_s[t, k, at, :]
                    for i in range(3):
                        part = force * (place[1 + dr, 1 + t + dc, i : i + 1, :] - home_place[t, i, at, :])
                        direct[i] = direct[i] + part
                        folded = part[0:8]
                        for q in range(8, CHUNK, 8):
                            folded = folded + part[q : q + 8]
                        partial[t, n, k, i] = folded
                for i in range(3):
                    sums[i, t, at, :] = direct[i]
                return carry
            lax.fori_loop(0, chunks, body, 0)
        ones = jnp.ones((8, points), f32)
        for row in range(3):
            for col in range(tiles + 2):
                for i in range(3):
                    total = None
                    for t in range(tiles):
                        for k, (dr, dc) in enumerate(STENCIL):
                            if (1 + dr, 1 + t + dc) == (row, col):
                                piece = jnp.sum(partial[t, :, k, i], axis=0)
                                total = piece if total is None else total + piece
                    total = -jnp.sum(total, axis=0, keepdims=True)
                    if row == 1 and 1 <= col <= tiles:
                        direct = lax.dot_general(
                            ones, sums[i, col - 1], (((1,), (1,)), ((), ())),
                            precision=lax.Precision.HIGHEST, preferred_element_type=f32,
                        )
                        total = total + direct[0:1]
                    result[row, col, i : i + 1, :] = total
                result[row, col, 3:4, :] = jnp.zeros((1, points), f32)

    def relax(t):
        def body(n, carry):
            at = pl.ds(pl.multiple_of(n * CHUNK, CHUNK), CHUNK)
            third = theta[t, at, :]
            for k in range(9):
                deviator = stretch_s[t, k, at, :] - third * length_s[t, k, at, :]
                for j, decay in enumerate((0.6, 0.95)):
                    back = decay * hist[j, 0, t, k, at, :].astype(f32) + (1.0 - decay) * deviator
                    hist[j, 0, t, k, at, :] = back.astype(hist.dtype)
            return carry
        lax.fori_loop(0, chunks, body, 0)

    measure(True)
    load_hist.wait()
    pull(pulls)
    start_all(WIDE, wide_copy)
    for t in range(tiles):
        relax(t)
    receive_all(WIDE, wide_copy)

    force = pulls[...]
    for n in range(len(WIDE)):
        force = force + wide_in[n]
    speed = halo[:, :, 8:12, :] + 0.2 * force
    moved = halo[:, :, 4:8, :] + 0.2 * speed
    place[...] = halo[:, :, 0:4, :] + moved
    speed = speed[1, 1 : 1 + tiles]
    moved = moved[1, 1 : 1 + tiles]
    for t in range(tiles):
        own = jnp.concatenate([place[1, 1 + t], jnp.zeros((4, points), f32)], axis=0)
        for i, wide in enumerate(over_lanes(own)):
            home_place[t, i] = wide

    measure(False)
    pull(last_pulls)
    start_all(NEAR, near_copy)
    stores = []
    for t in range(tiles):
        relax(t)
        for j in range(2):
            store = pltpu.make_async_copy(hist.at[j, 0, t], hist_out.at[j, 0, t], hist_out_sem.at[j, t])
            store.start()
            stores.append(store)
    receive_all(NEAR, near_copy)

    force = last_pulls[1, 1 : 1 + tiles]
    for n in range(len(NEAR)):
        force = force + near_in[n]
    speed = speed + 0.2 * force
    moved = moved + 0.2 * speed
    for t in range(tiles):
        for i in range(3):
            disp_out[i, 0, t : t + 1, :] = moved[t, i : i + 1, :]
            vel_out[i, 0, t : t + 1, :] = speed[t, i : i + 1, :]
    sent_all(NEAR, halo_copy)
    sent_all(WIDE, wide_copy)
    sent_all(NEAR, near_copy)
    for store in stores:
        store.wait()


def per_device(slabs, sections, rest_points, tile_fill, displacement, velocity, back_extension):
    _, rows, tiles, points = rest_points.shape
    assert rows == 1 and tiles >= 2
    f32 = jnp.float32
    vmem = pl.BlockSpec(memory_space=pltpu.VMEM)
    anywhere = pl.BlockSpec(memory_space=pl.ANY)
    bonds = (tiles, 9, points, points)
    dma = pltpu.SemaphoreType.DMA
    return pl.pallas_call(
        functools.partial(kernel, slabs, sections, tiles, points),
        out_shape=(
            jax.ShapeDtypeStruct(displacement.shape, f32),
            jax.ShapeDtypeStruct(velocity.shape, f32),
            jax.ShapeDtypeStruct(back_extension.shape, back_extension.dtype),
        ),
        in_specs=[vmem, vmem, vmem, vmem, anywhere],
        out_specs=(vmem, vmem, anywhere),
        scratch_shapes=[
            pltpu.VMEM(back_extension.shape, back_extension.dtype),
            pltpu.VMEM((3, tiles + 2, 16, points), f32),
            pltpu.VMEM((3, tiles + 2, 4, points), f32),
            pltpu.VMEM((3, tiles + 2, 4, points), f32),
            pltpu.VMEM((3, tiles + 2, 4, points), f32),
            pltpu.VMEM((len(WIDE), 3, tiles + 2, 4, points), f32),
            pltpu.VMEM((len(NEAR), tiles, 4, points), f32),
            pltpu.VMEM(bonds, f32),
            pltpu.VMEM(bonds, f32),
            pltpu.VMEM(bonds, f32),
            pltpu.VMEM(bonds, f32),
            pltpu.VMEM((tiles, 3, points, points), f32),
            pltpu.VMEM((tiles, 3, points, points), f32),
            pltpu.VMEM((3, tiles, points, points), f32),
            pltpu.VMEM((tiles, points, points), f32),
            pltpu.VMEM((tiles, points, points), f32),
            pltpu.VMEM((tiles, points // CHUNK, 9, 3, 8, points), f32),
            dma,
            dma((2, tiles)),
            dma((len(NEAR),)), dma((len(NEAR),)),
            dma((len(WIDE),)), dma((len(WIDE),)),
            dma((len(NEAR),)), dma((len(NEAR),)),
        ],
        compiler_params=pltpu.CompilerParams(
            collective_id=0, has_side_effects=True, vmem_limit_bytes=48 * 1024 * 1024
        ),
    )(rest_points, tile_fill, displacement, velocity, back_extension)


def solution(mesh):
    tiles = P(None, "slab", "col", None)
    states = P(None, "slab", "col", None, None, None)
    return jax.shard_map(
        functools.partial(per_device, mesh.shape["slab"], mesh.shape["col"]),
        mesh=mesh,
        in_specs=(tiles, P("slab", "col"), tiles, tiles, states),
        out_specs=(tiles, tiles, states),
        check_vma=False,
    )
```

time: 110 us -> 28.9 us (0.26)
  the two profiles are of different devices: /device:TPU:12 before, /device:TPU:1 now
where the time goes in v1:
time: 28.9 us; the launch traced here: 28.7 us
  Pallas kernels  21.9 us (76%)
  local copies, waits for them, and re-layouts  6.14 us (21%)
  between operations  0.65 us (2%)
    pallas_call x1, Pallas kernels, per_device(): pl.pallas_call(functools.partial(kernel, slabs, sections, tiles, points),...  21.9 us
    unnamed x13, local copies, waits for them, and re-layouts  6.14 us

profile of v1, /device:TPU:1, one launch (start us, length us, event | category | flops | bytes accessed | tf_op | source)
XLA Modules:
  0.0 28.7 jit_solution(8771639180624893095)
XLA Ops:
  0.6 0.0 copy-start
  0.6 1.3 %copy-done = bf16[2,1,2,9,128,128]{5,4,3,2,1,0:T(8,128)(2,1)S(1)} copy-done((bf16[2,1,2,9,128,128]{5,4,3,2,1,0:T(8,128)(2,1)S(1)}, bf16[2,1,2,9,128,128]{5,4,3,2,1,0:T(8,128)(2,1)}, u32[]{:S(2)}) %copy-start) | copy-done | bytes 1179672
  1.9 0.0 copy-start.1
  1.9 0.7 %copy-done.1 = f32[3,1,2,128]{3,2,1,0:T(2,128)S(1)} copy-done((f32[3,1,2,128]{3,2,1,0:T(2,128)S(1)}, f32[3,1,2,128]{3,2,1,0:T(2,128)}, u32[]{:S(2)}) %copy-start.1) | copy-done | bytes 3096
  2.6 0.0 copy-start.2
  2.6 0.7 %copy-done.2 = f32[3,1,2,128]{3,2,1,0:T(2,128)S(1)} copy-done((f32[3,1,2,128]{3,2,1,0:T(2,128)S(1)}, f32[3,1,2,128]{3,2,1,0:T(2,128)}, u32[]{:S(2)}) %copy-start.2) | copy-done | bytes 3096
  3.3 0.0 copy-start.3
  3.3 0.7 %copy-done.3 = f32[3,1,2,128]{3,2,1,0:T(2,128)S(1)} copy-done((f32[3,1,2,128]{3,2,1,0:T(2,128)S(1)}, f32[3,1,2,128]{3,2,1,0:T(2,128)}, u32[]{:S(2)}) %copy-start.3) | copy-done | bytes 3096
  4.0 0.0 copy-start.4
  4.0 0.7 %copy-done.4 = s32[1,2]{1,0:T(1,128)S(1)} copy-done((s32[1,2]{1,0:T(1,128)S(1)}, s32[1,2]{1,0:T(1,128)}, u32[]{:S(2)}) %copy-start.4) | copy-done | bytes 32
  4.6 21.9 %shard_map.76 = (f32[3,1,2,128]{3,2,1,0:T(2,128)S(1)}, f32[3,1,2,128]{3,2,1,0:T(2,128)S(1)}, bf16[2,1,2,9,128,128]{5,4,3,2,1,0:T(8,128)(2,1)S(1)}) custom-call(f32[3,1,2,128]{3,2,1,0:T(2,128)S(1)} %copy-done.1, s32[1,2]{1,0:T(1,128)S(1)} %copy-done.4, f32[3,1,2,128]{3,2,1,0:T(2,128)S(1)} %copy-done.2, f32[3,1,2,128]{3,2,1,0:T(2,128)S(1)} %copy-done.3, ...), custom_call_target="tpu_custom_call" | custom-call | tf_op jit(solution)/shard_map/pallas_call | solution.py:285
  26.5 0.6 %copy.11 = f32[3,1,2,128]{3,2,1,0:T(2,128)} copy(f32[3,1,2,128]{3,2,1,0:T(2,128)S(1)} %get-tuple-element.6) | data formatting | bytes 6144
  27.1 0.6 %copy.12 = f32[3,1,2,128]{3,2,1,0:T(2,128)} copy(f32[3,1,2,128]{3,2,1,0:T(2,128)S(1)} %get-tuple-element.7) | data formatting | bytes 6144
  27.7 1.0 %copy.13 = bf16[2,1,2,9,128,128]{5,4,3,2,1,0:T(8,128)(2,1)} copy(bf16[2,1,2,9,128,128]{5,4,3,2,1,0:T(8,128)(2,1)S(1)} %get-tuple-element.8) | data formatting | bytes 2359296
Async XLA Ops:
  0.6 1.3 %copy-start = (bf16[2,1,2,9,128,128]{5,4,3,2,1,0:T(8,128)(2,1)S(1)}, bf16[2,1,2,9,128,128]{5,4,3,2,1,0:T(8,128)(2,1)}, u32[]{:S(2)}) copy-start(bf16[2,1,2,9,128,128]{5,4,3,2,1,0:T(8,128)(2,1)} %hist_hbm.1) | copy-start | bytes 3538948
  1.9 0.7 %copy-start.1 = (f32[3,1,2,128]{3,2,1,0:T(2,128)S(1)}, f32[3,1,2,128]{3,2,1,0:T(2,128)}, u32[]{:S(2)}) copy-start(f32[3,1,2,128]{3,2,1,0:T(2,128)} %rest_ref.1) | copy-start | bytes 9220
  2.6 0.7 %copy-start.2 = (f32[3,1,2,128]{3,2,1,0:T(2,128)S(1)}, f32[3,1,2,128]{3,2,1,0:T(2,128)}, u32[]{:S(2)}) copy-start(f32[3,1,2,128]{3,2,1,0:T(2,128)} %disp_ref.1) | copy-start | bytes 9220
  3.3 0.7 %copy-start.3 = (f32[3,1,2,128]{3,2,1,0:T(2,128)S(1)}, f32[3,1,2,128]{3,2,1,0:T(2,128)}, u32[]{:S(2)}) copy-start(f32[3,1,2,128]{3,2,1,0:T(2,128)} %vel_ref.1) | copy-start | bytes 9220
  4.0 0.7 %copy-start.4 = (s32[1,2]{1,0:T(1,128)S(1)}, s32[1,2]{1,0:T(1,128)}, u32[]{:S(2)}) copy-start(s32[1,2]{1,0:T(1,128)} %fill_ref.1) | copy-start | bytes 28
